TPU v7x, 32 devices: a whole 2x2x4 slice. The times are simulated.
32 devices in a mesh: member: 2 (over x), space: 16 (over z, y, core).
Axes of the slice: x: 2, y: 2, z: 4, core: 2. Of those that a mesh axis runs over, the one named last changes fastest.
Arguments:
- state_field: bfloat16 [78, 64, 256], P(None, 'space'), may hold values from -6 to 6
- target_field: bfloat16 [78, 64, 256], P(None, 'space'), may hold values from -6 to 6
- noise_seeds: int32 [4], P('member'), may hold values from 0 to 999999
- first_weight: bfloat16 [9, 128, 86], replicated, may hold values from -0.21875 to 0.21875
- first_bias: float32 [128], replicated, may hold values from -3 to 3
- second_weight: bfloat16 [9, 78, 128], replicated, may hold values from -0.1875 to 0.1875
- second_bias: float32 [78], replicated, may hold values from -2 to 2
Outputs:
- state_gradient: float32 [78, 64, 256], P(None, 'space')
- first_weight_grad: float32 [9, 128, 86], replicated
- first_bias_grad: float32 [128], replicated
- second_weight_grad: float32 [9, 78, 128], replicated
- second_bias_grad: float32 [78], replicated
All inputs are finite; a program needn't handle non-finite values.
Results may differ from a plain program's by a relative error of at most 0.0039.
Values may be sent and summed in bfloat16 or wider, within the bound.
A program may use at most 64 MiB of HBM per device.

v0:
```python
import math

import jax
import jax.numpy as jnp
from jax import lax
from jax.sharding import PartitionSpec as P

SMOOTH_SQ = 0.01
TAP_STEPS = ((-1, -1), (-1, 0), (-1, 1), (0, -1), (0, 0), (0, 1), (1, -1), (1, 0), (1, 1))


def with_halo(array, sides, width):
    for axis, dim in sides:
        size, length = (lax.axis_size(axis), array.shape[dim])
        up = [(i, (i + 1) % size) for i in range(size - 1)]
        down = [(j, i) for i, j in up]
        last = lax.slice_in_dim(array, length - width, length, axis=dim)
        initial = lax.slice_in_dim(array, 0, width, axis=dim)
        before = lax.ppermute(last, axis, up)
        after = lax.ppermute(initial, axis, down)
        array = jnp.concatenate([before, array, after], axis=dim)
    return array


def smooth_slope(difference):
    return difference / jnp.sqrt(difference * difference + SMOOTH_SQ)


def silu_slope(pre_act):
    gate_value = jax.nn.sigmoid(pre_act)
    return gate_value * (1.0 + pre_act * (1.0 - gate_value))


def member_noise(seed_values, first_row, row_count, lon_count, channels):
    row_ids = (first_row + jnp.arange(row_count, dtype=jnp.int32))[None, None, :, None]
    lon_ids = jnp.arange(lon_count, dtype=jnp.int32)[None, None, None, :]
    chan_ids = jnp.arange(channels, dtype=jnp.int32)[None, :, None, None]
    seed_grid = seed_values[:, None, None, None]
    hashed = (seed_grid * 7 + row_ids * 1439 + lon_ids * 31 + chan_ids * 104729) % 65521
    folded = hashed % 46340
    mixed_hash = (folded * folded + chan_ids * 97 + lon_ids * 13) % 65521
    return mixed_hash.astype(jnp.float32) / 32760.0 - 1.0


def build_inputs(state_ext, seed_values, first_row, total_rows, noise_count):
    row_count = state_ext.shape[1]
    noise_field = member_noise(seed_values, first_row, row_count, state_ext.shape[2], noise_count)
    row_ids = first_row + jnp.arange(row_count, dtype=jnp.int32)
    inside = ((row_ids >= 0) & (row_ids < total_rows))[None, None, :, None]
    noise_field = jnp.where(inside, noise_field, 0.0).astype(jnp.bfloat16)
    repeated = jnp.broadcast_to(state_ext[None], (seed_values.shape[0],) + state_ext.shape)
    return jnp.concatenate([repeated, noise_field], axis=1)


def convolve(weight, padded, row_count):
    running = None
    for tap_index, (row_step, lon_step) in enumerate(TAP_STEPS):
        row_band = padded[:, :, 1 + row_step : 1 + row_step + row_count, :]
        tap_term = jnp.einsum(
            "oi,mirl->morl",
            weight[tap_index],
            jnp.roll(row_band, -lon_step, axis=3),
            preferred_element_type=jnp.float32,
        )
        running = tap_term if running is None else running + tap_term
    return running


def transposed_member(weight, padded, row_count):
    running = None
    for tap_index, (row_step, lon_step) in enumerate(TAP_STEPS):
        row_band = padded[:, :, 1 - row_step : 1 - row_step + row_count, :]
        tap_term = jnp.einsum(
            "oi,morl->mirl",
            weight[tap_index],
            jnp.roll(row_band, lon_step, axis=3),
            preferred_element_type=jnp.float32,
        )
        running = tap_term if running is None else running + tap_term
    return running


def transposed_summed(weight, padded, row_count):
    running = None
    for tap_index, (row_step, lon_step) in enumerate(TAP_STEPS):
        row_band = padded[:, :, 1 - row_step : 1 - row_step + row_count, :]
        tap_term = jnp.einsum(
            "oi,morl->irl",
            weight[tap_index],
            jnp.roll(row_band, lon_step, axis=3),
            preferred_element_type=jnp.float32,
        )
        running = tap_term if running is None else running + tap_term
    return running


def weight_grad(gradient, padded):
    row_count = gradient.shape[2]
    tap_terms = []
    for row_step, lon_step in TAP_STEPS:
        row_band = padded[:, :, 1 + row_step : 1 + row_step + row_count, :]
        tap_terms.append(
            jnp.einsum(
                "morl,mirl->oi",
                gradient,
                jnp.roll(row_band, -lon_step, axis=3),
                preferred_element_type=jnp.float32,
            )
        )
    return jnp.stack(tap_terms, axis=0)


def pair_total(own_values, everyone):

    def add_pair(member_index, running):
        partner = lax.dynamic_index_in_dim(everyone, member_index, 0, keepdims=False).astype(
            jnp.float32
        )
        return running + smooth_slope(own_values - partner[None])

    return lax.fori_loop(0, everyone.shape[0], add_pair, jnp.zeros(own_values.shape, jnp.float32))


def local(
    state_field, target_field, noise_seeds, first_weight, first_bias, second_weight, second_bias
):
    channels, row_count, lon_count = state_field.shape
    noise_count = first_weight.shape[2] - channels
    total_rows = row_count * lax.axis_size("space")
    first_row = lax.axis_index("space") * row_count
    members = noise_seeds.shape[0] * lax.axis_size("member")
    bias_one = first_bias[None, :, None, None]
    state_ext = with_halo(state_field, (("space", 1),), 1)
    inputs = build_inputs(state_ext, noise_seeds, first_row - 1, total_rows, noise_count)
    pre_own = bias_one + convolve(first_weight, inputs, row_count)
    hidden = jax.nn.silu(pre_own).astype(jnp.bfloat16)
    hidden_ext = with_halo(hidden, (("space", 2),), 1)
    state_wide = state_field.astype(jnp.float32)
    output_field = (
        state_wide[None]
        + second_bias[None, :, None, None]
        + convolve(second_weight, hidden_ext, row_count)
    ).astype(jnp.bfloat16)
    own_values = output_field.astype(jnp.float32)
    everyone = lax.all_gather(output_field, "member", axis=0, tiled=True)
    pair_sum = pair_total(own_values, everyone)
    own_rows = first_row + jnp.arange(row_count, dtype=jnp.int32)
    area_weight = jnp.sin(math.pi * (own_rows.astype(jnp.float32) + 0.5) / total_rows)[:, None]
    target_slope = smooth_slope(own_values - target_field.astype(jnp.float32)[None])
    out_grad = (
        area_weight * (target_slope / members - pair_sum / (members * (members - 1)))
    ).astype(jnp.bfloat16)
    grad_ext = with_halo(out_grad, (("space", 2),), 1)
    second_w_grad = weight_grad(out_grad, hidden_ext)
    second_b_grad = jnp.sum(out_grad.astype(jnp.float32), axis=(0, 2, 3))
    hidden_grad = transposed_member(second_weight, grad_ext, row_count)
    pre_grad = (hidden_grad * silu_slope(pre_own)).astype(jnp.bfloat16)
    first_b_grad = jnp.sum(pre_grad.astype(jnp.float32), axis=(0, 2, 3))
    first_w_grad = weight_grad(pre_grad, inputs)
    state_weight = first_weight[:, :, :channels]
    pre_ext = with_halo(pre_grad, (("space", 2),), 1)
    carried = transposed_summed(state_weight, pre_ext, row_count)
    state_local = jnp.sum(out_grad.astype(jnp.float32), axis=0) + carried
    state_gradient = lax.psum(state_local, "member")
    summed = lax.psum(
        (first_w_grad, first_b_grad, second_w_grad, second_b_grad), ("member", "space")
    )
    squares = (
        jnp.sum(summed[0] * summed[0])
        + jnp.sum(summed[1] * summed[1])
        + jnp.sum(summed[2] * summed[2])
        + jnp.sum(summed[3] * summed[3])
    )
    weight_count = summed[0].size + summed[1].size + summed[2].size + summed[3].size
    factor = jnp.minimum(1.0, math.sqrt(weight_count) / jnp.sqrt(squares))
    return (
        state_gradient,
        summed[0] * factor,
        summed[1] * factor,
        summed[2] * factor,
        summed[3] * factor,
    )


def solution(mesh):
    placed = (P(None, "space", None), P(None, "space", None), P("member"), P(), P(), P(), P())
    return jax.shard_map(
        local,
        mesh=mesh,
        in_specs=placed,
        out_specs=(P(None, "space", None), P(), P(), P(), P()),
        check_vma=False,
    )
```

profile of v0, /device:TPU:0, one launch (start us, length us, event | category | flops | bytes accessed | tf_op | source)
XLA Modules:
  0.0 253.4 jit_solution(14536071278774141697)
XLA Ops:
  7.2 1.1 fusion.259
  8.3 2.4 collective-permute-start
  10.7 1.3 collective-permute-start.1
  13.2 2.8 %collective-permute-done.1 = bf16[78,1,256]{2,1,0:T(2,128)(2,1)S(1)} collective-permute-done((bf16[78,1,256]{2,1,0:T(2,128)(2,1)S(1)}, bf16[78,1,256]{2,1,0:T(2,128)(2,1)S(1)}, u32[]{:S(2)}, u32[]{:S(2)}) %collective-permute-start.1) | collective-permute-done | bytes 39968 | tf_op jit(solution)/shard_map/ppermute | solution.py:20
  16.0 1.2 pad_maximum_fusion.34
  22.9 1.5 multiply_convert_fusion
  24.5 5.1 %collective-permute-start.2 = (bf16[2,128,1,256]{1,3,2,0:T(8,128)(2,1)S(1)}, bf16[2,128,1,256]{1,3,2,0:T(8,128)(2,1)S(1)}, u32[]{:S(2)}, u32[]{:S(2)}) collective-permute-start(bf16[2,128,1,256]{1,3,2,0:T(8,128)(2,1)S(1)} %get-tuple-element.180), channel_id=1, source_target_pairs={{0,1},{1,2},{2,3},{3,4},{4,5},{5,6},{6,7},{7,8},{8,9},{9,10},{10,1... | collective-permute-start | bytes 393224 | tf_op jit(solution)/shard_map/ppermute | solution.py:19
  29.6 1.3 collective-permute-start.3
  31.8 1.0 copy.46
  37.9 9.1 %all_gather.3 = bf16[4,78,4,256]{3,2,1,0:T(4,128)(2,1)} all-gather(bf16[2,78,4,256]{3,2,1,0:T(4,128)(2,1)S(1)} %copy.58), channel_id=1, replica_groups=mesh['member'=2,'space'=16] {'member'}, dimensions={0}, use_global_device_ids=true | all-gather | bytes 958464 | tf_op jit(solution)/shard_map/all_gather | solution.py:145
  46.9 5.8 %while.14 = (s32[]{:T(128)}, f32[2,78,4,256]{3,2,1,0:T(4,128)S(1)}, bf16[4,78,4,256]{3,2,1,0:T(4,128)(2,1)}, f32[2,78,4,256]{3,2,1,0:T(4,128)S(1)}, s32[]{:T(128)}, /*index=5*/s32[]{:T(128)}) while((s32[]{:T(128)}, f32[2,78,4,256]{3,2,1,0:T(4,128)S(1)}, bf16[4,78,4,256]{3,2,1,0:T(4,128)(2,1)}, f32[2,78,4,256]{3,2,1,0:T(4,128)S(1)}, ...), condition=%wide.region_1.2_spmd.clone, body=%wide.region_0.1_spmd.clone.sunk | while | flops 1038339 | bytes 2715739 | solution.py:121
  46.9 0.9 bitcast_convert_fusion.2
  48.4 0.9 bitcast_convert_fusion.2
  49.8 0.9 bitcast_convert_fusion.2
  51.3 0.9 bitcast_convert_fusion.2
  52.7 2.0 convert_reduce_fusion.10
  58.7 1.3 collective-permute-start.4
  60.0 4.6 %collective-permute-start.5 = (bf16[2,78,1,256]{3,1,2,0:T(8,128)(2,1)S(1)}, bf16[2,78,1,256]{3,1,2,0:T(8,128)(2,1)S(1)}, u32[]{:S(2)}, u32[]{:S(2)}) collective-permute-start(bf16[2,78,1,256]{3,1,2,0:T(8,128)(2,1)S(1)} %get-tuple-element.199), channel_id=1, source_target_pairs={{0,1},{1,2},{2,3},{3,4},{4,5},{5,6},{6,7},{7,8},{8,9},{9,10},{10,1... | collective-permute-start | bytes 239624 | tf_op jit(solution)/shard_map/ppermute | solution.py:19
  76.7 3.7 %collective-permute-start.7 = (bf16[2,128,1,256]{1,3,2,0:T(8,128)(2,1)}, bf16[2,128,1,256]{1,3,2,0:T(8,128)(2,1)S(1)}, u32[]{:S(2)}, u32[]{:S(2)}) collective-permute-start(bf16[2,128,1,256]{1,3,2,0:T(8,128)(2,1)} %get-tuple-element.170), channel_id=1, source_target_pairs={{0,1},{1,2},{2,3},{3,4},{4,5},{5,6},{6,7},{7,8},{8,9},{9,10},{10,1... | collective-permute-start | bytes 393224 | tf_op jit(solution)/shard_map/ppermute | solution.py:19
  80.3 1.3 collective-permute-start.6
  82.8 2.5 collective-permute-done.6
  85.8 0.9 fusion.157
  86.7 1.4 convert_reduce_fusion.2
  88.2 46.0 %all-reduce = (f32[128]{0:T(128)S(1)}, f32[78]{0:T(128)S(1)}) all-reduce(f32[128]{0:T(128)S(1)} %get-tuple-element.123, f32[78]{0:T(128)S(1)} %copy-done.47), channel_id=1, replica_groups=mesh['member'=2,'space'=16] {'member','space'}, use_global_device_ids=true, to_apply=%region_16.17 | all-reduce | flops 206 | bytes 1648 | tf_op jit(solution)/shard_map/psum | solution.py:165
  134.2 1.2 convolution_add_fusion.22
  139.4 0.9 fusion.18
  140.4 78.5 %all-reduce.7.cloned.1.call-done = (f32[9,128,86]{1,2,0:T(8,128)}, f32[9,78,128]{2,1,0:T(8,128)}) async-done(((f32[9,128,86]{1,2,0:T(8,128)}, f32[9,78,128]{2,1,0:T(8,128)}), (f32[9,128,86]{1,2,0:T(8,128)}, f32[9,78,128]{2,1,0:T(8,128)})) %all-reduce.7.cloned.1.call-update) | async-done | bytes 755728 | tf_op jit(solution)/shard_map/psum | solution.py:165
  218.9 1.7 multiply_reduce_fusion.1
  220.6 1.7 multiply_reduce_fusion
  225.5 1.8 broadcast_multiply_fusion.1
  228.6 16.1 %all-reduce.5.cloned.1.call-done = f32[78,4,256]{2,0,1:T(8,128)} async-done(((f32[78,4,256]{2,0,1:T(8,128)}), f32[78,4,256]{2,0,1:T(8,128)}) %all-reduce.5.cloned.1.call-update) | async-done | bytes 319504 | tf_op jit(solution)/shard_map/psum | solution.py:164
  244.7 1.9 copy.88
  (201 shorter events, 37.5 us)
Async XLA Ops:
  7.2 211.7 %all-reduce.7.cloned.1.call-start = ((), (), s32[]{:S(2)}) async-start(), calls=%async_computation.1 | async-start | bytes 1548288 | tf_op jit(solution)/shard_map/psum | solution.py:165
  8.3 4.8 %collective-permute-start = (bf16[78,1,256]{2,1,0:T(2,128)(2,1)S(1)}, bf16[78,1,256]{2,1,0:T(2,128)(2,1)S(1)}, u32[]{:S(2)}, u32[]{:S(2)}) collective-permute-start(bf16[78,1,256]{2,1,0:T(2,128)(2,1)S(1)} %get-tuple-element.200), channel_id=1, source_target_pairs={{0,1},{1,2},{2,3},{3,4},{4,5},{5,6},{6,7},{7,8},{8,9},{9,10},{10,1... | collective-permute-start | bytes 119816 | tf_op jit(solution)/shard_map/ppermute | solution.py:19
  10.7 5.3 %collective-permute-start.1 = (bf16[78,1,256]{2,1,0:T(2,128)(2,1)S(1)}, bf16[78,1,256]{2,1,0:T(2,128)(2,1)S(1)}, u32[]{:S(2)}, u32[]{:S(2)}) collective-permute-start(bf16[78,1,256]{2,1,0:T(2,128)(2,1)S(1)} %get-tuple-element.201), channel_id=1, source_target_pairs={{1,0},{2,1},{3,2},{4,3},{5,4},{6,5},{7,6},{8,7},{9,8},{10,9},{11,1... | collective-permute-start | bytes 119816 | tf_op jit(solution)/shard_map/ppermute | solution.py:20
  17.6 2.2 copy-start.28
  17.6 2.6 %copy-start.26 = (bf16[2,86,4,1]{3,1,2,0:T(8,128)(2,1)}, bf16[2,86,4,1]{3,1,2,0:T(8,128)(2,1)S(1)}, u32[]{:S(2)}) copy-start(bf16[2,86,4,1]{3,1,2,0:T(8,128)(2,1)S(1)} %get-tuple-element.159) | copy-start | bytes 4132
  17.6 3.6 %copy-start.24 = (bf16[2,86,4,1]{3,1,2,0:T(8,128)(2,1)}, bf16[2,86,4,1]{3,1,2,0:T(8,128)(2,1)S(1)}, u32[]{:S(2)}) copy-start(bf16[2,86,4,1]{3,1,2,0:T(8,128)(2,1)S(1)} %get-tuple-element.160) | copy-start | bytes 4132
  17.6 4.1 %copy-start.22 = (bf16[2,86,4,1]{3,1,2,0:T(8,128)(2,1)}, bf16[2,86,4,1]{3,1,2,0:T(8,128)(2,1)S(1)}, u32[]{:S(2)}) copy-start(bf16[2,86,4,1]{3,1,2,0:T(8,128)(2,1)S(1)} %get-tuple-element.161) | copy-start | bytes 4132
  17.6 5.0 %copy-start.37 = (bf16[2,86,4,1]{3,1,2,0:T(8,128)(2,1)}, bf16[2,86,4,1]{3,1,2,0:T(8,128)(2,1)S(1)}, u32[]{:S(2)}) copy-start(bf16[2,86,4,1]{3,1,2,0:T(8,128)(2,1)S(1)} %get-tuple-element.156) | copy-start | bytes 4132
  18.2 1.6 copy-start.2
  18.2 2.1 copy-start
  18.2 4.5 %copy-start.31 = (bf16[2,86,4,255]{3,1,2,0:T(8,128)(2,1)}, bf16[2,86,4,255]{3,1,2,0:T(8,128)(2,1)S(1)}, u32[]{:S(2)}) copy-start(bf16[2,86,4,255]{3,1,2,0:T(8,128)(2,1)S(1)} %get-tuple-element.150) | copy-start | bytes 1052644
  22.9 8.0 %copy-start.33 = (bf16[78,4,256]{2,1,0:T(4,128)(2,1)S(1)}, bf16[78,4,256]{2,1,0:T(4,128)(2,1)}, u32[]{:S(2)}) copy-start(bf16[78,4,256]{2,1,0:T(4,128)(2,1)} %param.9) | copy-start | bytes 479236
  22.9 8.0 %copy-start.46 = (f32[78]{0:T(128)S(1)}, f32[78]{0:T(128)}, u32[]{:S(2)}) copy-start(f32[78]{0:T(128)} %param.15) | copy-start | bytes 940
  24.5 8.4 %copy-start.45 = (bf16[78,4,256]{2,1,0:T(4,128)(2,1)S(1)}, bf16[78,4,256]{2,1,0:T(4,128)(2,1)}, u32[]{:S(2)}) copy-start(bf16[78,4,256]{2,1,0:T(4,128)(2,1)} %param.10) | copy-start | bytes 479236
  24.5 9.2 %collective-permute-start.2 = (bf16[2,128,1,256]{1,3,2,0:T(8,128)(2,1)S(1)}, bf16[2,128,1,256]{1,3,2,0:T(8,128)(2,1)S(1)}, u32[]{:S(2)}, u32[]{:S(2)}) collective-permute-start(bf16[2,128,1,256]{1,3,2,0:T(8,128)(2,1)S(1)} %get-tuple-element.180), channel_id=1, source_target_pairs={{0,1},{1,2},{2,3},{3,4},{4,5},{5,6},{6,7},{7,8},{8,9},{9,10},{10,1... | collective-permute-start | bytes 393224 | tf_op jit(solution)/shard_map/ppermute | solution.py:19
  29.6 4.1 %collective-permute-start.3 = (bf16[2,128,1,256]{1,3,2,0:T(8,128)(2,1)S(1)}, bf16[2,128,1,256]{1,3,2,0:T(8,128)(2,1)S(1)}, u32[]{:S(2)}, u32[]{:S(2)}) collective-permute-start(bf16[2,128,1,256]{1,3,2,0:T(8,128)(2,1)S(1)} %get-tuple-element.181), channel_id=1, source_target_pairs={{1,0},{2,1},{3,2},{4,3},{5,4},{6,5},{7,6},{8,7},{9,8},{10,9},{11,1... | collective-permute-start | bytes 393224 | tf_op jit(solution)/shard_map/ppermute | solution.py:20
  34.2 1.7 copy-start.16
  34.2 2.0 copy-start.6
  34.2 2.4 copy-start.8
  34.2 3.0 %copy-start.14 = (bf16[2,128,4,255]{1,3,2,0:T(8,128)(2,1)}, bf16[2,128,4,255]{1,3,2,0:T(8,128)(2,1)S(1)}, u32[]{:S(2)}) copy-start(bf16[2,128,4,255]{1,3,2,0:T(8,128)(2,1)S(1)} %get-tuple-element.146) | copy-start | bytes 1566724
  52.7 2.0 copy-start.40
  57.7 6.9 %copy-start.15 = (bf16[2,128,4,255]{1,3,2,0:T(8,128)(2,1)S(1)}, bf16[2,128,4,255]{1,3,2,0:T(8,128)(2,1)}, u32[]{:S(2)}) copy-start(bf16[2,128,4,255]{1,3,2,0:T(8,128)(2,1)} %copy-done.14) | copy-start | bytes 1566724
  58.7 7.6 %collective-permute-start.4 = (bf16[2,78,1,256]{3,1,2,0:T(8,128)(2,1)S(1)}, bf16[2,78,1,256]{3,1,2,0:T(8,128)(2,1)S(1)}, u32[]{:S(2)}, u32[]{:S(2)}) collective-permute-start(bf16[2,78,1,256]{3,1,2,0:T(8,128)(2,1)S(1)} %get-tuple-element.198), channel_id=1, source_target_pairs={{1,0},{2,1},{3,2},{4,3},{5,4},{6,5},{7,6},{8,7},{9,8},{10,9},{11,1... | collective-permute-start | bytes 239624 | tf_op jit(solution)/shard_map/ppermute | solution.py:20
  60.0 7.0 %collective-permute-start.5 = (bf16[2,78,1,256]{3,1,2,0:T(8,128)(2,1)S(1)}, bf16[2,78,1,256]{3,1,2,0:T(8,128)(2,1)S(1)}, u32[]{:S(2)}, u32[]{:S(2)}) collective-permute-start(bf16[2,78,1,256]{3,1,2,0:T(8,128)(2,1)S(1)} %get-tuple-element.199), channel_id=1, source_target_pairs={{0,1},{1,2},{2,3},{3,4},{4,5},{5,6},{6,7},{7,8},{8,9},{9,10},{10,1... | collective-permute-start | bytes 239624 | tf_op jit(solution)/shard_map/ppermute | solution.py:19
  76.1 5.6 %copy-start.32 = (bf16[2,86,4,255]{3,1,2,0:T(8,128)(2,1)S(1)}, bf16[2,86,4,255]{3,1,2,0:T(8,128)(2,1)}, u32[]{:S(2)}) copy-start(bf16[2,86,4,255]{3,1,2,0:T(8,128)(2,1)} %copy-done.31) | copy-start | bytes 1052644
  76.1 5.6 %copy-start.38 = (bf16[2,86,4,1]{3,1,2,0:T(8,128)(2,1)S(1)}, bf16[2,86,4,1]{3,1,2,0:T(8,128)(2,1)}, u32[]{:S(2)}) copy-start(bf16[2,86,4,1]{3,1,2,0:T(8,128)(2,1)} %copy-done.37) | copy-start | bytes 4132
  76.7 6.2 %collective-permute-start.7 = (bf16[2,128,1,256]{1,3,2,0:T(8,128)(2,1)}, bf16[2,128,1,256]{1,3,2,0:T(8,128)(2,1)S(1)}, u32[]{:S(2)}, u32[]{:S(2)}) collective-permute-start(bf16[2,128,1,256]{1,3,2,0:T(8,128)(2,1)} %get-tuple-element.170), channel_id=1, source_target_pairs={{0,1},{1,2},{2,3},{3,4},{4,5},{5,6},{6,7},{7,8},{8,9},{9,10},{10,1... | collective-permute-start | bytes 393224 | tf_op jit(solution)/shard_map/ppermute | solution.py:19
  80.3 4.9 %collective-permute-start.6 = (bf16[2,128,1,256]{1,3,2,0:T(8,128)(2,1)S(1)}, bf16[2,128,1,256]{1,3,2,0:T(8,128)(2,1)S(1)}, u32[]{:S(2)}, u32[]{:S(2)}) collective-permute-start(bf16[2,128,1,256]{1,3,2,0:T(8,128)(2,1)S(1)} %get-tuple-element.171), channel_id=1, source_target_pairs={{1,0},{2,1},{3,2},{4,3},{5,4},{6,5},{7,6},{8,7},{9,8},{10,9},{11,1... | collective-permute-start | bytes 393224 | tf_op jit(solution)/shard_map/ppermute | solution.py:20
  82.8 161.9 %all-reduce.5.cloned.1.call-start = ((), (), s32[]{:S(2)}) async-start(), calls=%async_computation | async-start | bytes 655360 | tf_op jit(solution)/shard_map/psum | solution.py:164
  88.2 47.2 %copy-start.36 = (bf16[128,4,256]{0,2,1:T(8,128)(2,1)S(1)}, bf16[128,4,256]{0,2,1:T(8,128)(2,1)}, u32[]{:S(2)}) copy-start(bf16[128,4,256]{0,2,1:T(8,128)(2,1)} %get-tuple-element.125) | copy-start | bytes 786436
  88.2 47.2 %copy-start.42 = (bf16[9,128,86]{1,2,0:T(8,128)(2,1)S(1)}, bf16[9,128,86]{1,2,0:T(8,128)(2,1)}, u32[]{:S(2)}) copy-start(bf16[9,128,86]{1,2,0:T(8,128)(2,1)} %param.12) | copy-start | bytes 594436
  218.9 8.9 %copy-start.30 = (f32[9,128,86]{1,2,0:T(8,128)S(1)}, f32[9,128,86]{1,2,0:T(8,128)}, u32[]{:S(2)}) copy-start(f32[9,128,86]{1,2,0:T(8,128)} %get-tuple-element.139) | copy-start | bytes 1188868
  (28 other events, 29.9 us)
Sparse Core Ops, SparseCore 0:
  82.9 135.9 all-reduce.6
  221.3 23.3 all-reduce.4
where the time goes:
time: 255 us; the launch traced here: 253 us
  waiting for transfers between devices  100 us (39%)
  blocking collectives  55 us (22%)
  other arithmetic  23.2 us (9%)
  matrix products  21.6 us (8%)
  starting transfers between devices  21 us (8%)
  between operations  17.7 us (7%)
  local copies, waits for them, and re-layouts  14.7 us (6%)
    psum x1, waiting for transfers between devices, local(): lax.psum((first_w_grad, first_b_grad, second_w_grad, second_b_grad), ('me...  78.5 us
    psum x1, blocking collectives, local(): lax.psum((first_w_grad, first_b_grad, second_w_grad, second_b_grad), ('me...  46 us
    psum x1, waiting for transfers between devices, local(): state_gradient = lax.psum(state_local, 'member')  16.1 us
    ppermute x4, starting transfers between devices, with_halo(): before = lax.ppermute(last, axis, up)  15.8 us
    unnamed x102, local copies, waits for them, and re-layouts  10.9 us
    all_gather x1, blocking collectives, local(): everyone = lax.all_gather(output_field, 'member', axis=0, tiled=True)  9.09 us
    dot_general x18, matrix products, convolve(): jnp.einsum('oi,mirl->morl', weight[tap_index], jnp.roll(row_band, -lon_st...  8.05 us
    ppermute x4, waiting for transfers between devices, with_halo(): after = lax.ppermute(initial, axis, down)  5.31 us
  transfers between devices with their start and end apart: 10, of which 4 were waited for; matrix products, arithmetic and copies ran while one was open for 8% of the time, Pallas kernels for 0%

commit v1 on v0

v1 whole, which is shorter than its diff:
```python
import functools
import math

import jax
import jax.numpy as jnp
from jax import lax
from jax.experimental import pallas as pl
from jax.experimental.pallas import tpu as pltpu
from jax.sharding import PartitionSpec as P

SMOOTH_SQ = 0.01
MESH = pl.DeviceIdType.MESH
F32 = jnp.float32
BF16 = jnp.bfloat16
NT = (((1,), (1,)), ((), ()))


def modulo(value, divisor):
    quotient = (value.astype(F32) * (1.0 / divisor)).astype(jnp.int32)
    left = value - quotient * divisor
    left = jnp.where(left < 0, left + divisor, left)
    return jnp.where(left >= divisor, left - divisor, left)


def slope(diff):
    return diff * lax.rsqrt(diff * diff + SMOOTH_SQ)


def dot(a, b):
    return jnp.dot(a, b, preferred_element_type=F32)


def dot_nt(a, b):
    return lax.dot_general(a, b, NT, preferred_element_type=F32)


def kernel(
    space_size, cfg,
    fields, seeds, aux, w1s, w1n, b1, w2f, b2, w2t, w1t,
    grads_out, state_out,
    ext, all_seeds, xs3, xn3, pre_common, h3, gate, outs, og3, pg3, total, recv1, send2, recv2, send3, recv3, recv4, part4,
    gathered,
    halo_send, halo_recv, seed_sem, state_sem, red_send, red_recv, gat_send, gat_recv, more_send, more_recv,
):
    C, CP, HID, LON, BAND, MEM, NOISE = cfg
    own = BAND // 2
    s = lax.axis_index("space")
    h = lax.axis_index("member")
    has_left = s > 0
    has_right = s < space_size - 1
    bits = (space_size.bit_length() - 1) - 4
    core = s % 2
    quad = h * 2 + (s // 2) % 2
    quad_y = (s // 2) % 2
    zed = (s // 4) % 4

    def flip(value, mask, unit, width):
        digit = (value // unit) % width
        flipped = jnp.int32(0)
        place = 1
        while place < width:
            bit = (digit // place) % 2
            if mask & place:
                bit = 1 - bit
            flipped = flipped + bit * place
            place *= 2
        return value + (flipped - digit) * unit

    def at(member, space):
        return (member, space)

    core_peer = at(h, flip(s, 1, 1, 2))
    member_peer = at(1 - h, s)
    quad_peers = []
    for d in (1, 2, 3):
        quad_peers.append(at(1 - h if d & 2 else h, flip(s, 1, 2, 2) if d & 1 else s))
    zed_peers = [at(h, flip(s, d, 4, 4)) for d in (1, 2, 3)]
    far_peers = [at(h, flip(s, 1, 16 << k, 2)) for k in range(bits)]

    barrier = pltpu.get_barrier_semaphore()
    fixed = [core_peer, member_peer] + quad_peers + zed_peers + far_peers
    for peer in fixed:
        pl.semaphore_signal(barrier, inc=1, device_id=peer, device_id_type=MESH)

    @pl.when(has_left)
    def _():
        pl.semaphore_signal(barrier, inc=1, device_id=at(h, s - 1), device_id_type=MESH)

    @pl.when(has_right)
    def _():
        pl.semaphore_signal(barrier, inc=1, device_id=at(h, s + 1), device_id_type=MESH)

    pl.semaphore_wait(
        barrier, len(fixed) + has_left.astype(jnp.int32) + has_right.astype(jnp.int32)
    )

    width = BAND * LON
    to_left = pltpu.make_async_remote_copy(
        src_ref=fields, dst_ref=ext.at[:, 2 * width : 3 * width],
        send_sem=halo_send.at[0], recv_sem=halo_recv.at[0],
        device_id=at(h, s - 1), device_id_type=MESH,
    )
    to_right = pltpu.make_async_remote_copy(
        src_ref=fields, dst_ref=ext.at[:, 0:width],
        send_sem=halo_send.at[1], recv_sem=halo_recv.at[1],
        device_id=at(h, s + 1), device_id_type=MESH,
    )
    swap = pltpu.make_async_remote_copy(
        src_ref=seeds, dst_ref=all_seeds.at[h],
        send_sem=seed_sem.at[0], recv_sem=seed_sem.at[1],
        device_id=member_peer, device_id_type=MESH,
    )
    swap.start()

    @pl.when(has_left)
    def _():
        to_left.start()

    @pl.when(has_right)
    def _():
        to_right.start()

    all_seeds[h] = seeds[...]
    ext[:, width : 2 * width] = fields[...]
    total[...] = jnp.zeros_like(total)

    @pl.when(jnp.logical_not(has_left))
    def _():
        ext[:, 0:width] = jnp.zeros((2 * CP, width), BF16)

    @pl.when(jnp.logical_not(has_right))
    def _():
        ext[:, 2 * width : 3 * width] = jnp.zeros((2 * CP, width), BF16)

    swap.wait()

    n_in = 2 * own + 6
    base_row = s * BAND + h * own - 4
    lon = lax.broadcasted_iota(jnp.int32, (NOISE, LON), 1)
    chan = lax.broadcasted_iota(jnp.int32, (NOISE, LON), 0)
    lane_term = lon * 31 + chan * 104729
    late_term = chan * 97 + lon * 13

    def noise_member(m, carry):
        seed = all_seeds[m // 2, pl.ds(m % 2, 1), :]
        seed7 = jnp.concatenate([seed, seed], axis=1) * 7
        for j in range(10):
            hashed = modulo(jnp.maximum(seed7 + (base_row + j) * 1439 + lane_term, 0), 65521)
            folded = jnp.where(hashed >= 46340, hashed - 46340, hashed)
            mixed = modulo(folded * folded + late_term, 65521)
            value = mixed.astype(F32) / 32760.0 - 1.0
            value = value * aux[8 + j : 9 + j, :]
            value = value.astype(BF16).astype(F32)
            zero = jnp.zeros_like(value)
            for b, shift in enumerate((1, 0, LON - 1)):
                moved = pltpu.roll(value, shift, 1) if shift else value
                xn3[m, b * 16 : b * 16 + 16, j * LON : (j + 1) * LON] = jnp.concatenate(
                    [moved, zero], axis=0
                ).astype(BF16)
        return carry

    lax.fori_loop(0, MEM, noise_member, 0)

    @pl.when(has_left)
    def _():
        to_left.wait_send()
        to_right.wait_recv()

    @pl.when(has_right)
    def _():
        to_right.wait_send()
        to_left.wait_recv()

    def ext_cols(j):
        return pl.ds(pl.multiple_of(h * (own * LON), own * LON) + j * LON, LON)

    row_of = lax.broadcasted_iota(jnp.int32, (CP, LON), 0)
    for j in range(10):
        value = ext[0:CP, ext_cols(j)].astype(F32)
        for b, shift in enumerate((1, 0, LON - 1)):
            moved = pltpu.roll(value, shift, 1) if shift else jnp.where(row_of == C, 1.0, value)
            xs3[b * CP : (b + 1) * CP, j * LON : (j + 1) * LON] = moved.astype(BF16)

    def cols(j, n=1):
        return slice(j * LON, (j + n) * LON)

    for k in range(8):
        pre_common[:, cols(k)] = (
            dot(w1s[0], xs3[:, cols(k)])
            + dot(w1s[1], xs3[:, cols(k + 1)])
            + dot(w1s[2], xs3[:, cols(k + 2)])
            + b1[...]
        )

    def forward(m, carry):
        for k in range(8):
            noise9 = jnp.concatenate([xn3[m, :, cols(k + a)] for a in range(3)], axis=0)
            pre = pre_common[:, cols(k)] + dot(w1n[...], noise9)
            sig = 1.0 / (1.0 + jnp.exp(-pre))
            hid = pre * sig * aux[9 + k : 10 + k, :]
            hid = hid.astype(BF16).astype(F32)
            if 2 <= k < 6:
                gate[m, :, cols(k - 2)] = sig * (1.0 + pre * (1.0 - sig)) * aux[9 + k : 10 + k, :]
            for b, shift in enumerate((1, 0, LON - 1)):
                moved = pltpu.roll(hid, shift, 1) if shift else hid
                h3[m, b * HID : (b + 1) * HID, cols(k)] = moved.astype(BF16)
        for n in range(6):
            hid9 = jnp.concatenate([h3[m, :, cols(n + a)] for a in range(3)], axis=0)
            state = ext[0:CP, ext_cols(n + 2)].astype(F32)
            outs[m, :, cols(n)] = (state + b2[...] + dot(w2f[...], hid9)).astype(BF16)
        return carry

    lax.fori_loop(0, MEM, forward, 0)

    for n in range(6):
        values = [outs[m, :, cols(n)].astype(F32) for m in range(MEM)]
        target = ext[CP : 2 * CP, ext_cols(n + 2)].astype(F32)
        sums = [jnp.zeros((CP, LON), F32)] * MEM
        for m in range(MEM):
            for q in range(m + 1, MEM):
                term = slope(values[m] - values[q])
                sums[m] = sums[m] + term
                sums[q] = sums[q] - term
        for m in range(MEM):
            grad = aux[n : n + 1, :] * (
                slope(values[m] - target) * (1.0 / MEM) - sums[m] * (1.0 / (MEM * (MEM - 1)))
            )
            grad = grad.astype(BF16).astype(F32)
            for b, shift in enumerate((LON - 1, 0, 1)):
                moved = pltpu.roll(grad, shift, 1) if shift else grad
                og3[m, b * CP : (b + 1) * CP, cols(n)] = moved.astype(BF16)

    first_row = jnp.where(
        lax.broadcasted_iota(jnp.int32, (8, own * LON), 0) == 0, 1.0, 0.0
    ).astype(BF16)
    per_tap = CP + NOISE
    second = 9 * per_tap
    keep_c = lax.broadcasted_iota(jnp.int32, (CP, HID), 0) < C

    def backward(m, carry):
        for p in range(4):
            hidden_grad = (
                dot(w2t[0], og3[m, :, cols(p + 2)])
                + dot(w2t[1], og3[m, :, cols(p + 1)])
                + dot(w2t[2], og3[m, :, cols(p)])
            )
            grad = (hidden_grad * gate[m, :, cols(p)]).astype(BF16).astype(F32)
            for b, shift in enumerate((LON - 1, 0, 1)):
                moved = pltpu.roll(grad, shift, 1) if shift else grad
                pg3[m, b * HID : (b + 1) * HID, cols(p)] = moved.astype(BF16)
        own_out = og3[m, CP : 2 * CP, cols(2, own)]
        own_pre = pg3[m, HID : 2 * HID, cols(1, own)]
        for a in range(3):
            part = dot_nt(own_out, h3[m, :, cols(2 + a, own)])
            first_s = dot_nt(xs3[:, cols(3 + a, own)], own_pre)
            first_n = dot_nt(xn3[m, :, cols(3 + a, own)], own_pre)
            for b in range(3):
                tap = 3 * a + b
                at_row = second + tap * CP
                total[at_row : at_row + CP, :] += part[:, b * HID : (b + 1) * HID]
                chunk = first_s[b * CP : (b + 1) * CP]
                if tap != 4:
                    chunk = jnp.where(keep_c, chunk, 0.0)
                total[tap * per_tap : tap * per_tap + CP, :] += chunk
                total[tap * per_tap + CP : (tap + 1) * per_tap, :] += first_n[
                    b * 16 : b * 16 + NOISE
                ]
        at_row = second + 9 * CP
        total[at_row : at_row + 8, 0:CP] += dot_nt(first_row, own_out)
        return carry

    lax.fori_loop(0, MEM, backward, 0)

    rows = total.shape[0]
    half, quarter, piece = rows // 2, rows // 8, rows // 32
    keep1 = pl.multiple_of(core * half, half)
    away1 = pl.multiple_of((1 - core) * half, half)
    first_copy = pltpu.make_async_remote_copy(
        src_ref=total.at[pl.ds(away1, half)], dst_ref=recv1,
        send_sem=red_send.at[0], recv_sem=red_recv.at[0],
        device_id=core_peer, device_id_type=MESH,
    )
    first_copy.start()

    for t in range(own):
        value = jnp.zeros((CP, LON), F32)
        for m in range(MEM):
            grad9 = jnp.concatenate([pg3[m, :, cols(t + 2 - a)] for a in range(3)], axis=0)
            value = value + dot(w1t[...], grad9)
            value = value + og3[m, CP : 2 * CP, cols(t + 2)].astype(F32)
        state_out[h, :, cols(t)] = value
    state_copy = pltpu.make_async_remote_copy(
        src_ref=state_out.at[h], dst_ref=state_out.at[h],
        send_sem=state_sem.at[0], recv_sem=state_sem.at[1],
        device_id=member_peer, device_id_type=MESH,
    )

    first_copy.wait()
    total[pl.ds(keep1, half), :] += recv1[...]
    send2[...] = total[pl.ds(keep1, half), :].astype(BF16)
    copies = []
    for d in (1, 2, 3):
        qm = 1 - h if d & 2 else h
        qy = 1 - quad_y if d & 1 else quad_y
        start = pl.multiple_of((qm * 2 + qy) * quarter, quarter)
        copies.append(pltpu.make_async_remote_copy(
            src_ref=send2.at[pl.ds(start, quarter)], dst_ref=recv2.at[d - 1],
            send_sem=red_send.at[d], recv_sem=red_recv.at[d],
            device_id=quad_peers[d - 1], device_id_type=MESH,
        ))
        copies[-1].start()
    state_copy.start()
    for copy in copies:
        copy.wait()
    keep2 = pl.multiple_of(keep1 + quad * quarter, quarter)
    value = total[pl.ds(keep2, quarter), :]
    for d in range(3):
        value = value + recv2[d].astype(F32)
    total[pl.ds(keep2, quarter), :] = value
    send3[...] = value.astype(BF16)
    copies = []
    for d in (1, 2, 3):
        other = flip(zed, d, 1, 4)
        start = pl.multiple_of(other * piece, piece)
        copies.append(pltpu.make_async_remote_copy(
            src_ref=send3.at[pl.ds(start, piece)], dst_ref=recv3.at[d - 1],
            send_sem=red_send.at[3 + d], recv_sem=red_recv.at[3 + d],
            device_id=zed_peers[d - 1], device_id_type=MESH,
        ))
        copies[-1].start()
    for copy in copies:
        copy.wait()
    keep3 = pl.multiple_of(keep2 + zed * piece, piece)
    value = total[pl.ds(keep3, piece), :]
    for d in range(3):
        value = value + recv3[d].astype(F32)
    for k in range(bits):
        part4[k] = value
        copy = pltpu.make_async_remote_copy(
            src_ref=part4.at[k], dst_ref=recv4.at[k],
            send_sem=more_send.at[k], recv_sem=more_recv.at[k],
            device_id=far_peers[k], device_id_type=MESH,
        )
        copy.start()
        copy.wait()
        value = value + recv4[k]
    gathered[pl.ds(keep3, piece), :] = value.astype(BF16)

    slot = 0
    for start, size, peers in (
        (keep3, piece, zed_peers), (keep2, quarter, quad_peers), (keep1, half, [core_peer])
    ):
        copies = []
        for peer in peers:
            copies.append(pltpu.make_async_remote_copy(
                src_ref=gathered.at[pl.ds(start, size)], dst_ref=gathered.at[pl.ds(start, size)],
                send_sem=gat_send.at[slot], recv_sem=gat_recv.at[slot],
                device_id=peer, device_id_type=MESH,
            ))
            copies[-1].start()
            slot += 1
        for copy in copies:
            copy.wait()

    everything = gathered[...].astype(F32)
    squares = jnp.sum(everything * everything)
    count = 9 * HID * (C + NOISE) + HID + 9 * C * HID + C
    norm = jnp.sqrt(jnp.broadcast_to(squares, (8, HID)))
    factor = jnp.minimum(1.0, math.sqrt(count) / norm)
    grads_out[...] = everything * factor[0:1, :]
    state_copy.wait()


def local(
    state_field, target_field, noise_seeds, first_weight, first_bias, second_weight, second_bias
):
    C, band, lon = state_field.shape
    hid = first_weight.shape[1]
    noise = first_weight.shape[2] - C
    space_size = lax.axis_size("space")
    members = noise_seeds.shape[0] * lax.axis_size("member")
    total_rows = band * space_size
    cp = (C + 1 + 15) // 16 * 16
    own = band // 2
    fields = jnp.pad(
        jnp.stack([state_field, target_field]), ((0, 0), (0, cp - C), (0, 0), (0, 0))
    ).reshape(2 * cp, band * lon)
    seeds = jnp.broadcast_to(
        jnp.pad(noise_seeds, (0, 8 - noise_seeds.shape[0]))[:, None], (8, 128)
    )
    base = lax.axis_index("space") * band + lax.axis_index("member") * own
    row_ids = base - 4 + jnp.arange(10, dtype=jnp.int32)
    inside = ((row_ids >= 0) & (row_ids < total_rows)).astype(F32)
    out_ids = row_ids[2:8]
    area = jnp.sin(math.pi * (out_ids.astype(F32) + 0.5) / total_rows) * inside[2:8]
    aux = jnp.concatenate([area, jnp.zeros((2,), F32), inside, jnp.zeros((6,), F32)])
    aux = jnp.broadcast_to(aux[:, None], (24, lon))
    w1_state = jnp.pad(first_weight[:, :, :C], ((0, 0), (0, 0), (0, cp - C)))
    w1_noise = jnp.pad(first_weight[:, :, C:], ((0, 0), (0, 0), (0, 16 - noise)))
    w2 = jnp.pad(second_weight, ((0, 0), (0, cp - C), (0, 0)))
    w1s = w1_state.reshape(3, 3, hid, cp).transpose(0, 2, 1, 3).reshape(3, hid, 3 * cp)
    w1n = w1_noise.transpose(1, 0, 2).reshape(hid, 9 * 16)
    w2f = w2.transpose(1, 0, 2).reshape(cp, 9 * hid)
    w2t = w2.reshape(3, 3, cp, hid).transpose(0, 3, 1, 2).reshape(3, hid, 3 * cp)
    w1t = w1_state.transpose(2, 0, 1).reshape(cp, 9 * hid)
    b1 = first_bias[:, None]
    b2 = jnp.pad(second_bias, (0, cp - C))[:, None]
    per_tap = cp + noise
    used = 9 * per_tap + 9 * cp + 8
    rows = (used + 511) // 512 * 512
    half, quarter, piece = rows // 2, rows // 8, rows // 32
    far = max(1, space_size.bit_length() - 5)
    vmem = pl.BlockSpec(memory_space=pltpu.VMEM)
    dma = pltpu.SemaphoreType.DMA
    cfg = (C, cp, hid, lon, band, members, noise)
    grads, state = pl.pallas_call(
        functools.partial(kernel, space_size, cfg),
        out_shape=(
            jax.ShapeDtypeStruct((rows, hid), F32),
            jax.ShapeDtypeStruct((2, cp, own * lon), F32),
        ),
        in_specs=[vmem] * 10,
        out_specs=(vmem, vmem),
        scratch_shapes=[
            pltpu.VMEM((2 * cp, 3 * band * lon), BF16),
            pltpu.VMEM((2, 8, 128), jnp.int32),
            pltpu.VMEM((3 * cp, 10 * lon), BF16),
            pltpu.VMEM((members, 48, 10 * lon), BF16),
            pltpu.VMEM((hid, 8 * lon), F32),
            pltpu.VMEM((members, 3 * hid, 8 * lon), BF16),
            pltpu.VMEM((members, hid, 4 * lon), F32),
            pltpu.VMEM((members, cp, 6 * lon), BF16),
            pltpu.VMEM((members, 3 * cp, 6 * lon), BF16),
            pltpu.VMEM((members, 3 * hid, 4 * lon), BF16),
            pltpu.VMEM((rows, hid), F32),
            pltpu.VMEM((half, hid), F32),
            pltpu.VMEM((half, hid), BF16),
            pltpu.VMEM((3, quarter, hid), BF16),
            pltpu.VMEM((quarter, hid), BF16),
            pltpu.VMEM((3, piece, hid), BF16),
            pltpu.VMEM((far, piece, hid), F32),
            pltpu.VMEM((far, piece, hid), F32),
            pltpu.VMEM((rows, hid), BF16),
            dma((2,)), dma((2,)), dma((2,)), dma((2,)),
            dma((7,)), dma((7,)), dma((7,)), dma((7,)), dma((far,)), dma((far,)),
        ],
        compiler_params=pltpu.CompilerParams(
            collective_id=0, has_side_effects=True, vmem_limit_bytes=48 * 1024 * 1024
        ),
    )(fields, seeds, aux, w1s, w1n, b1, w2f, b2, w2t, w1t)
    state_gradient = state.reshape(2, cp, own, lon)[:, :C].transpose(1, 0, 2, 3).reshape(
        C, band, lon
    )
    first = grads[: 9 * per_tap].reshape(9, per_tap, hid)
    first_w = jnp.concatenate([first[:, :C], first[:, cp:]], axis=1).transpose(0, 2, 1)
    first_b = first[4, C]
    second = grads[9 * per_tap : 9 * per_tap + 9 * cp].reshape(9, cp, hid)[:, :C]
    second_b = grads[9 * per_tap + 9 * cp, :C]
    return state_gradient, first_w, first_b, second, second_b


def solution(mesh):
    placed = (P(None, "space", None), P(None, "space", None), P("member"), P(), P(), P(), P())
    return jax.shard_map(
        local,
        mesh=mesh,
        in_specs=placed,
        out_specs=(P(None, "space", None), P(), P(), P(), P()),
        check_vma=False,
    )
```

time: 255 us -> 55.9 us (0.22)
  waiting for transfers between devices: 100 us -> 0 us
  blocking collectives: 55 us -> 0 us
  Pallas kernels: 0 us -> 45.8 us
  other arithmetic: 23.2 us -> 1.23 us
  matrix products: 21.6 us -> 0 us
  starting transfers between devices: 21 us -> 0 us
  between operations: 17.7 us -> 0.81 us
  local copies, waits for them, and re-layouts: 14.7 us -> 7.82 us
    psum x2 -> x0, waiting for transfers between devices: 94.7 us -> none  [the longest x1 78.5 us: local(): lax.psum((first_w_grad, first_b_grad, second_w_grad, second_b_grad), ('me...]
    psum x1 -> x0, blocking collectives: 46 us -> none  [local(): lax.psum((first_w_grad, first_b_grad, second_w_grad, second_b_grad), ('me...]
    pallas_call x0 -> x1, Pallas kernels: none -> 45.8 us  [local(): pl.pallas_call(functools.partial(kernel, space_size, cfg), out_shape=(jax...]
    dot_general x54 -> x0, matrix products: 21.6 us -> none  [the longest x18 8.05 us: convolve(): jnp.einsum('oi,mirl->morl', weight[tap_index], jnp.roll(row_band, -lon_st...]
    ppermute x8 -> x0, starting transfers between devices: 21 us -> none  [the longest x4 15.8 us: with_halo(): before = lax.ppermute(last, axis, up)]
    all_gather x1 -> x0, blocking collectives: 9.09 us -> none  [local(): everyone = lax.all_gather(output_field, 'member', axis=0, tiled=True)]
    reduce_sum x10 -> x0, other arithmetic: 8.51 us -> none  [the longest x1 1.98 us: local(): second_b_grad = jnp.sum(out_grad.astype(jnp.float32), axis=(0, 2, 3))]
    unnamed x102 -> x17, local copies, waits for them, and re-layouts: 10.9 us -> 2.88 us
  transfers between devices with their start and end apart: 10 -> 0, of which waited for: 4 -> 0; matrix products, arithmetic and copies ran while one was open for 8% -> 0% of each run, Pallas kernels for 0% -> 0%
where the time goes in v1:
time: 55.9 us; the launch traced here: 55.7 us
  Pallas kernels  45.8 us (82%)
  local copies, waits for them, and re-layouts  7.82 us (14%)
  other arithmetic  1.23 us (2%)
  between operations  0.81 us (1%)
    pallas_call x1, Pallas kernels, local(): pl.pallas_call(functools.partial(kernel, space_size, cfg), out_shape=(jax...  45.8 us
    unnamed x17, local copies, waits for them, and re-layouts  2.88 us
    reshape x2, local copies, waits for them, and re-layouts, local(): state.reshape(2, cp, own, lon)[:, :C].transpose(1, 0, 2, 3)  1.21 us

profile of v1, /device:TPU:0, one launch (start us, length us, event | category | flops | bytes accessed | tf_op | source)
XLA Modules:
  0.0 55.7 jit_solution(11958773220727594569)
XLA Ops:
  0.7 0.0 copy-start.6
  0.7 0.1 slice_multiply_fusion
  0.8 0.5 copy-done.6
  1.3 0.6 %copy-done.7 = f32[78]{0:T(128)S(1)} copy-done((f32[78]{0:T(128)S(1)}, f32[78]{0:T(128)}, u32[]{:S(2)}) %copy-start.7) | copy-done | bytes 336
  2.0 0.1 pad_maximum_fusion
  2.1 0.1 broadcast_in_dim.8.seeds
  2.1 0.8 %slice.40 = bf16[9,128,8]{1,2,0:T(8,128)(2,1)S(1)} slice(bf16[9,128,86]{1,2,0:T(8,128)(2,1)} %param.10), slice={[0:9], [0:128], [78:86]} | slice | bytes 36864 | tf_op jit(solution)/shard_map/slice | solution.py:399
  3.0 0.1 broadcast_in_dim.9.aux
  3.1 0.1 copy.23.w1n
  3.2 0.1 copy.25.b2
  3.3 0.0 copy-done.4
  3.3 0.1 copy.24.b1
  3.4 0.0 copy-done.2
  3.4 0.1 fusion.2
  3.6 0.0 copy-start.1
  3.6 0.9 %copy-done.1 = bf16[9,78,128]{2,1,0:T(8,128)(2,1)S(1)} copy-done((bf16[9,78,128]{2,1,0:T(8,128)(2,1)S(1)}, bf16[9,78,128]{2,1,0:T(8,128)(2,1)}, u32[]{:S(2)}) %copy-start.1) | copy-done | bytes 179736
  4.5 0.1 fusion.4
  4.5 0.0 copy-start
  4.5 0.0 copy-start.5
  4.6 0.1 copy.26.w2t
  4.7 0.8 %copy-done = bf16[9,128,86]{1,2,0:T(8,128)(2,1)S(1)} copy-done((bf16[9,128,86]{1,2,0:T(8,128)(2,1)S(1)}, bf16[9,128,86]{1,2,0:T(8,128)(2,1)}, u32[]{:S(2)}) %copy-start) | copy-done | bytes 198168
  5.5 0.1 fusion.3
  5.6 0.1 copy.22.w1s
  5.8 45.8 %shard_map.110 = (f32[1536,128]{1,0:T(8,128)S(1)}, f32[2,80,512]{2,1,0:T(8,128)S(1)}) custom-call(bf16[160,1024]{1,0:T(8,128)(2,1)S(1)} %bitcast.42, s32[8,128]{1,0:T(8,128)S(1)} %broadcast_in_dim.8.seeds, f32[24,256]{1,0:T(8,128)S(1)} %broadcast_in_dim.9.aux, bf16[3,128,240]{2,1,0:T(8,128)(2,1)S(1)} %copy.22.w1s, bf16[128,144]{1,0:T(8,128)(2,1)S(1)} %copy.23.w1n, ...), custom_call_target="tpu_custom_call" | custom-call | tf_op jit(solution)/shard_map/pallas_call | solution.py:416
  51.6 0.2 reshape.56
  51.8 0.1 slice_bitcast_fusion
  51.9 0.1 copy.27
  52.0 1.0 %reshape.57 = f32[78,4,256]{2,1,0:T(4,128)} reshape(f32[78,2,2,256]{3,2,1,0:T(2,128)S(1)} %copy.27) | data formatting | bytes 638976 | tf_op jit(solution)/shard_map/reshape | solution.py:451
  53.0 0.5 slice_bitcast_fusion.2
  53.5 0.8 %slice.46 = f32[720,128]{1,0:T(8,128)} slice(f32[1536,128]{1,0:T(8,128)S(1)} %get-tuple-element.8), slice={[792:1512], [0:128]} | slice | bytes 737280 | tf_op jit(solution)/shard_map/slice | solution.py:457
  54.3 0.5 slice_bitcast_fusion.1
  54.9 0.8 %maximum_bitcast_fusion = f32[9,128,86]{1,2,0:T(8,128)} fusion(f32[9,8,128]{2,1,0:T(8,128)S(1)} %slice.51, f32[9,78,128]{2,1,0:T(8,128)S(1)} %slice.50), kind=kLoop, calls=%fused_computation.3 | loop fusion | flops 99072 | bytes 792576 | tf_op jit(solution)/shard_map/transpose | solution.py:455
  (18 shorter events, 0.2 us)
Async XLA Ops:
  0.7 0.7 %copy-start.6 = (s32[2]{0:T(128)S(1)}, s32[2]{0:T(128)}, u32[]{:S(2)}) copy-start(s32[2]{0:T(128)} %param.9) | copy-start | bytes 28
  1.3 0.7 %copy-start.7 = (f32[78]{0:T(128)S(1)}, f32[78]{0:T(128)}, u32[]{:S(2)}) copy-start(f32[78]{0:T(128)} %param.13) | copy-start | bytes 940
  2.1 1.2 %copy-start.4 = (f32[128]{0:T(128)S(1)}, f32[128]{0:T(128)}, u32[]{:S(2)}) copy-start(f32[128]{0:T(128)} %param.11) | copy-start | bytes 1540
  2.1 1.3 %copy-start.2 = (bf16[78,4,256]{2,1,0:T(4,128)(2,1)S(1)}, bf16[78,4,256]{2,1,0:T(4,128)(2,1)}, u32[]{:S(2)}) copy-start(bf16[78,4,256]{2,1,0:T(4,128)(2,1)} %param.8) | copy-start | bytes 479236
  2.1 1.3 %copy-start.3 = (bf16[78,4,256]{2,1,0:T(4,128)(2,1)S(1)}, bf16[78,4,256]{2,1,0:T(4,128)(2,1)}, u32[]{:S(2)}) copy-start(bf16[78,4,256]{2,1,0:T(4,128)(2,1)} %param.7) | copy-start | bytes 479236
  3.6 0.9 %copy-start.1 = (bf16[9,78,128]{2,1,0:T(8,128)(2,1)S(1)}, bf16[9,78,128]{2,1,0:T(8,128)(2,1)}, u32[]{:S(2)}) copy-start(bf16[9,78,128]{2,1,0:T(8,128)(2,1)} %param.12) | copy-start | bytes 539140
  4.5 0.9 %copy-start = (bf16[9,128,86]{1,2,0:T(8,128)(2,1)S(1)}, bf16[9,128,86]{1,2,0:T(8,128)(2,1)}, u32[]{:S(2)}) copy-start(bf16[9,128,86]{1,2,0:T(8,128)(2,1)} %param.10) | copy-start | bytes 594436
  4.5 0.9 %copy-start.5 = (pred[80]{0:T(512)(128)(4,1)S(1)}, pred[80]{0:T(512)(128)(4,1)}, u32[]{:S(2)}) copy-start(pred[80]{0:T(512)(128)(4,1)} %constant.34.clone.1) | copy-start | bytes 244

commit v2 on v1

--- a/solution.py
+++ b/solution.py
@@ -90,50 +90,7 @@
     def _():
         pl.semaphore_signal(barrier, inc=1, device_id=at(h, s + 1), device_id_type=MESH)
 
-    pl.semaphore_wait(
-        barrier, len(fixed) + has_left.astype(jnp.int32) + has_right.astype(jnp.int32)
-    )
-
-    width = BAND * LON
-    to_left = pltpu.make_async_remote_copy(
-        src_ref=fields, dst_ref=ext.at[:, 2 * width : 3 * width],
-        send_sem=halo_send.at[0], recv_sem=halo_recv.at[0],
-        device_id=at(h, s - 1), device_id_type=MESH,
-    )
-    to_right = pltpu.make_async_remote_copy(
-        src_ref=fields, dst_ref=ext.at[:, 0:width],
-        send_sem=halo_send.at[1], recv_sem=halo_recv.at[1],
-        device_id=at(h, s + 1), device_id_type=MESH,
-    )
-    swap = pltpu.make_async_remote_copy(
-        src_ref=seeds, dst_ref=all_seeds.at[h],
-        send_sem=seed_sem.at[0], recv_sem=seed_sem.at[1],
-        device_id=member_peer, device_id_type=MESH,
-    )
-    swap.start()
-
-    @pl.when(has_left)
-    def _():
-        to_left.start()
-
-    @pl.when(has_right)
-    def _():
-        to_right.start()
-
     all_seeds[h] = seeds[...]
-    ext[:, width : 2 * width] = fields[...]
-    total[...] = jnp.zeros_like(total)
-
-    @pl.when(jnp.logical_not(has_left))
-    def _():
-        ext[:, 0:width] = jnp.zeros((2 * CP, width), BF16)
-
-    @pl.when(jnp.logical_not(has_right))
-    def _():
-        ext[:, 2 * width : 3 * width] = jnp.zeros((2 * CP, width), BF16)
-
-    swap.wait()
-
     n_in = 2 * own + 6
     base_row = s * BAND + h * own - 4
     lon = lax.broadcasted_iota(jnp.int32, (NOISE, LON), 1)
@@ -159,7 +116,51 @@
                 ).astype(BF16)
         return carry
 
-    lax.fori_loop(0, MEM, noise_member, 0)
+    each = MEM // 2
+    lax.fori_loop(h * each, h * each + each, noise_member, 0)
+    pl.semaphore_wait(
+        barrier, len(fixed) + has_left.astype(jnp.int32) + has_right.astype(jnp.int32)
+    )
+
+    width = BAND * LON
+    to_left = pltpu.make_async_remote_copy(
+        src_ref=fields, dst_ref=ext.at[:, 2 * width : 3 * width],
+        send_sem=halo_send.at[0], recv_sem=halo_recv.at[0],
+        device_id=at(h, s - 1), device_id_type=MESH,
+    )
+    to_right = pltpu.make_async_remote_copy(
+        src_ref=fields, dst_ref=ext.at[:, 0:width],
+        send_sem=halo_send.at[1], recv_sem=halo_recv.at[1],
+        device_id=at(h, s + 1), device_id_type=MESH,
+    )
+    swap = pltpu.make_async_remote_copy(
+        src_ref=seeds, dst_ref=all_seeds.at[h],
+        send_sem=seed_sem.at[0], recv_sem=seed_sem.at[1],
+        device_id=member_peer, device_id_type=MESH,
+    )
+    swap.start()
+
+    @pl.when(has_left)
+    def _():
+        to_left.start()
+
+    @pl.when(has_right)
+    def _():
+        to_right.start()
+
+    ext[:, width : 2 * width] = fields[...]
+    total[...] = jnp.zeros_like(total)
+
+    @pl.when(jnp.logical_not(has_left))
+    def _():
+        ext[:, 0:width] = jnp.zeros((2 * CP, width), BF16)
+
+    @pl.when(jnp.logical_not(has_right))
+    def _():
+        ext[:, 2 * width : 3 * width] = jnp.zeros((2 * CP, width), BF16)
+
+    swap.wait()
+    lax.fori_loop((1 - h) * each, (1 - h) * each + each, noise_member, 0)
 
     @pl.when(has_left)
     def _():
@@ -248,6 +249,26 @@
             for b, shift in enumerate((LON - 1, 0, 1)):
                 moved = pltpu.roll(grad, shift, 1) if shift else grad
                 pg3[m, b * HID : (b + 1) * HID, cols(p)] = moved.astype(BF16)
+        return carry
+
+    lax.fori_loop(0, MEM, backward, 0)
+
+    for t in range(own):
+        value = jnp.zeros((CP, LON), F32)
+        for m in range(MEM):
+            grad9 = jnp.concatenate([pg3[m, :, cols(t + 2 - a)] for a in range(3)], axis=0)
+            value = value + dot(w1t[...], grad9)
+            value = value + og3[m, CP : 2 * CP, cols(t + 2)].astype(F32)
+        state_out[h, :, cols(t)] = value
+    state_copy = pltpu.make_async_remote_copy(
+        src_ref=state_out.at[h], dst_ref=state_out.at[h],
+        send_sem=state_sem.at[0], recv_sem=state_sem.at[1],
+        device_id=member_peer, device_id_type=MESH,
+    )
+
+    state_copy.start()
+
+    def weights(m, carry):
         own_out = og3[m, CP : 2 * CP, cols(2, own)]
         own_pre = pg3[m, HID : 2 * HID, cols(1, own)]
         for a in range(3):
@@ -269,7 +290,7 @@
         total[at_row : at_row + 8, 0:CP] += dot_nt(first_row, own_out)
         return carry
 
-    lax.fori_loop(0, MEM, backward, 0)
+    lax.fori_loop(0, MEM, weights, 0)
 
     rows = total.shape[0]
     half, quarter, piece = rows // 2, rows // 8, rows // 32
@@ -281,19 +302,6 @@
         device_id=core_peer, device_id_type=MESH,
     )
     first_copy.start()
-
-    for t in range(own):
-        value = jnp.zeros((CP, LON), F32)
-        for m in range(MEM):
-            grad9 = jnp.concatenate([pg3[m, :, cols(t + 2 - a)] for a in range(3)], axis=0)
-            value = value + dot(w1t[...], grad9)
-            value = value + og3[m, CP : 2 * CP, cols(t + 2)].astype(F32)
-        state_out[h, :, cols(t)] = value
-    state_copy = pltpu.make_async_remote_copy(
-        src_ref=state_out.at[h], dst_ref=state_out.at[h],
-        send_sem=state_sem.at[0], recv_sem=state_sem.at[1],
-        device_id=member_peer, device_id_type=MESH,
-    )
 
     first_copy.wait()
     total[pl.ds(keep1, half), :] += recv1[...]
@@ -309,7 +317,6 @@
             device_id=quad_peers[d - 1], device_id_type=MESH,
         ))
         copies[-1].start()
-    state_copy.start()
     for copy in copies:
         copy.wait()
     keep2 = pl.multiple_of(keep1 + quad * quarter, quarter)

time: 55.9 us -> 57.4 us (1.027)
  Pallas kernels: 45.8 us -> 47.3 us
    pallas_call x1, Pallas kernels: 45.8 us -> 47.3 us  [local(): pl.pallas_call(functools.partial(kernel, space_size, cfg), out_shape=(jax...]
where the time goes in v2:
time: 57.4 us; the launch traced here: 57.2 us
  Pallas kernels  47.3 us (82%)
  local copies, waits for them, and re-layouts  7.82 us (14%)
  other arithmetic  1.23 us (2%)
  between operations  0.81 us (1%)
    pallas_call x1, Pallas kernels, local(): pl.pallas_call(functools.partial(kernel, space_size, cfg), out_shape=(jax...  47.3 us
    unnamed x17, local copies, waits for them, and re-layouts  2.88 us
    reshape x2, local copies, waits for them, and re-layouts, local(): state.reshape(2, cp, own, lon)[:, :C].transpose(1, 0, 2, 3)  1.21 us

profile of v2, /device:TPU:0, one launch (start us, length us, event | category | flops | bytes accessed | tf_op | source)
XLA Modules:
  0.0 57.2 jit_solution(8801965079293364237)
XLA Ops:
  0.7 0.0 copy-start.6
  0.7 0.1 slice_multiply_fusion
  0.8 0.5 copy-done.6
  1.3 0.6 %copy-done.7 = f32[78]{0:T(128)S(1)} copy-done((f32[78]{0:T(128)S(1)}, f32[78]{0:T(128)}, u32[]{:S(2)}) %copy-start.7) | copy-done | bytes 336
  2.0 0.1 pad_maximum_fusion
  2.1 0.1 broadcast_in_dim.8.seeds
  2.1 0.8 %slice.40 = bf16[9,128,8]{1,2,0:T(8,128)(2,1)S(1)} slice(bf16[9,128,86]{1,2,0:T(8,128)(2,1)} %param.10), slice={[0:9], [0:128], [78:86]} | slice | bytes 36864 | tf_op jit(solution)/shard_map/slice | solution.py:406
  3.0 0.1 broadcast_in_dim.9.aux
  3.1 0.1 copy.23.w1n
  3.2 0.1 copy.25.b2
  3.3 0.0 copy-done.4
  3.3 0.1 copy.24.b1
  3.4 0.0 copy-done.2
  3.4 0.1 fusion.2
  3.6 0.0 copy-start.1
  3.6 0.9 %copy-done.1 = bf16[9,78,128]{2,1,0:T(8,128)(2,1)S(1)} copy-done((bf16[9,78,128]{2,1,0:T(8,128)(2,1)S(1)}, bf16[9,78,128]{2,1,0:T(8,128)(2,1)}, u32[]{:S(2)}) %copy-start.1) | copy-done | bytes 179736
  4.5 0.1 fusion.4
  4.5 0.0 copy-start
  4.5 0.0 copy-start.5
  4.6 0.1 copy.26.w2t
  4.7 0.8 %copy-done = bf16[9,128,86]{1,2,0:T(8,128)(2,1)S(1)} copy-done((bf16[9,128,86]{1,2,0:T(8,128)(2,1)S(1)}, bf16[9,128,86]{1,2,0:T(8,128)(2,1)}, u32[]{:S(2)}) %copy-start) | copy-done | bytes 198168
  5.5 0.1 fusion.3
  5.6 0.1 copy.22.w1s
  5.8 47.3 %shard_map.110 = (f32[1536,128]{1,0:T(8,128)S(1)}, f32[2,80,512]{2,1,0:T(8,128)S(1)}) custom-call(bf16[160,1024]{1,0:T(8,128)(2,1)S(1)} %bitcast.42, s32[8,128]{1,0:T(8,128)S(1)} %broadcast_in_dim.8.seeds, f32[24,256]{1,0:T(8,128)S(1)} %broadcast_in_dim.9.aux, bf16[3,128,240]{2,1,0:T(8,128)(2,1)S(1)} %copy.22.w1s, bf16[128,144]{1,0:T(8,128)(2,1)S(1)} %copy.23.w1n, ...), custom_call_target="tpu_custom_call" | custom-call | tf_op jit(solution)/shard_map/pallas_call | solution.py:423
  53.1 0.2 reshape.56
  53.3 0.1 slice_bitcast_fusion
  53.4 0.1 copy.27
  53.6 1.0 %reshape.57 = f32[78,4,256]{2,1,0:T(4,128)} reshape(f32[78,2,2,256]{3,2,1,0:T(2,128)S(1)} %copy.27) | data formatting | bytes 638976 | tf_op jit(solution)/shard_map/reshape | solution.py:458
  54.5 0.5 slice_bitcast_fusion.2
  55.1 0.8 %slice.46 = f32[720,128]{1,0:T(8,128)} slice(f32[1536,128]{1,0:T(8,128)S(1)} %get-tuple-element.8), slice={[792:1512], [0:128]} | slice | bytes 737280 | tf_op jit(solution)/shard_map/slice | solution.py:464
  55.9 0.5 slice_bitcast_fusion.1
  56.4 0.8 %maximum_bitcast_fusion = f32[9,128,86]{1,2,0:T(8,128)} fusion(f32[9,8,128]{2,1,0:T(8,128)S(1)} %slice.51, f32[9,78,128]{2,1,0:T(8,128)S(1)} %slice.50), kind=kLoop, calls=%fused_computation.3 | loop fusion | flops 99072 | bytes 792576 | tf_op jit(solution)/shard_map/transpose | solution.py:462
  (18 shorter events, 0.2 us)
Async XLA Ops:
  0.7 0.7 %copy-start.6 = (s32[2]{0:T(128)S(1)}, s32[2]{0:T(128)}, u32[]{:S(2)}) copy-start(s32[2]{0:T(128)} %param.9) | copy-start | bytes 28
  1.3 0.7 %copy-start.7 = (f32[78]{0:T(128)S(1)}, f32[78]{0:T(128)}, u32[]{:S(2)}) copy-start(f32[78]{0:T(128)} %param.13) | copy-start | bytes 940
  2.1 1.2 %copy-start.4 = (f32[128]{0:T(128)S(1)}, f32[128]{0:T(128)}, u32[]{:S(2)}) copy-start(f32[128]{0:T(128)} %param.11) | copy-start | bytes 1540
  2.1 1.3 %copy-start.2 = (bf16[78,4,256]{2,1,0:T(4,128)(2,1)S(1)}, bf16[78,4,256]{2,1,0:T(4,128)(2,1)}, u32[]{:S(2)}) copy-start(bf16[78,4,256]{2,1,0:T(4,128)(2,1)} %param.8) | copy-start | bytes 479236
  2.1 1.3 %copy-start.3 = (bf16[78,4,256]{2,1,0:T(4,128)(2,1)S(1)}, bf16[78,4,256]{2,1,0:T(4,128)(2,1)}, u32[]{:S(2)}) copy-start(bf16[78,4,256]{2,1,0:T(4,128)(2,1)} %param.7) | copy-start | bytes 479236
  3.6 0.9 %copy-start.1 = (bf16[9,78,128]{2,1,0:T(8,128)(2,1)S(1)}, bf16[9,78,128]{2,1,0:T(8,128)(2,1)}, u32[]{:S(2)}) copy-start(bf16[9,78,128]{2,1,0:T(8,128)(2,1)} %param.12) | copy-start | bytes 539140
  4.5 0.9 %copy-start = (bf16[9,128,86]{1,2,0:T(8,128)(2,1)S(1)}, bf16[9,128,86]{1,2,0:T(8,128)(2,1)}, u32[]{:S(2)}) copy-start(bf16[9,128,86]{1,2,0:T(8,128)(2,1)} %param.10) | copy-start | bytes 594436
  4.5 0.9 %copy-start.5 = (pred[80]{0:T(512)(128)(4,1)S(1)}, pred[80]{0:T(512)(128)(4,1)}, u32[]{:S(2)}) copy-start(pred[80]{0:T(512)(128)(4,1)} %constant.34.clone.1) | copy-start | bytes 244

commit v3 on v1

--- a/solution.py
+++ b/solution.py
@@ -95,16 +95,50 @@
     )
 
     width = BAND * LON
-    to_left = pltpu.make_async_remote_copy(
-        src_ref=fields, dst_ref=ext.at[:, 2 * width : 3 * width],
-        send_sem=halo_send.at[0], recv_sem=halo_recv.at[0],
-        device_id=at(h, s - 1), device_id_type=MESH,
-    )
-    to_right = pltpu.make_async_remote_copy(
-        src_ref=fields, dst_ref=ext.at[:, 0:width],
-        send_sem=halo_send.at[1], recv_sem=halo_recv.at[1],
-        device_id=at(h, s + 1), device_id_type=MESH,
-    )
+    near = own * LON
+    left_far, right_far = 2 * width, 0
+
+    def halo(slot, low, source, target, space):
+        return pltpu.make_async_remote_copy(
+            src_ref=fields.at[low : low + CP, source : source + near],
+            dst_ref=ext.at[low : low + CP, target : target + near],
+            send_sem=halo_send.at[slot], recv_sem=halo_recv.at[slot],
+            device_id=at(h, space), device_id_type=MESH,
+        )
+
+    left_near = [halo(0, 0, 0, left_far, s - 1)]
+    right_near = [halo(1, 0, near, right_far + near, s + 1)]
+    right_more = [halo(2, 0, 0, right_far, s + 1), halo(3, CP, near, right_far + near, s + 1)]
+    left_more = [halo(4, 0, near, left_far + near, s - 1), halo(5, CP, 0, left_far, s - 1)]
+    lower = h == 0
+    upper = jnp.logical_not(lower)
+    sends = (
+        (has_left, left_near), (has_right, right_near),
+        (has_left & upper, left_more), (has_right & lower, right_more),
+    )
+    arrivals = (
+        (has_right, left_near), (has_left, right_near),
+        (has_right & upper, left_more), (has_left & lower, right_more),
+    )
+
+    def start_all(group):
+        def run():
+            for copy in group:
+                copy.start()
+        return run
+
+    def await_sent(group):
+        def run():
+            for copy in group:
+                copy.wait_send()
+        return run
+
+    def await_arrived(group):
+        def run():
+            for copy in group:
+                copy.wait_recv()
+        return run
+
     swap = pltpu.make_async_remote_copy(
         src_ref=seeds, dst_ref=all_seeds.at[h],
         send_sem=seed_sem.at[0], recv_sem=seed_sem.at[1],
@@ -112,13 +146,8 @@
     )
     swap.start()
 
-    @pl.when(has_left)
-    def _():
-        to_left.start()
-
-    @pl.when(has_right)
-    def _():
-        to_right.start()
+    for condition, group in sends:
+        pl.when(condition)(start_all(group))
 
     all_seeds[h] = seeds[...]
     ext[:, width : 2 * width] = fields[...]
@@ -161,15 +190,10 @@
 
     lax.fori_loop(0, MEM, noise_member, 0)
 
-    @pl.when(has_left)
-    def _():
-        to_left.wait_send()
-        to_right.wait_recv()
-
-    @pl.when(has_right)
-    def _():
-        to_right.wait_send()
-        to_left.wait_recv()
+    for condition, group in sends:
+        pl.when(condition)(await_sent(group))
+    for condition, group in arrivals:
+        pl.when(condition)(await_arrived(group))
 
     def ext_cols(j):
         return pl.ds(pl.multiple_of(h * (own * LON), own * LON) + j * LON, LON)
@@ -441,7 +465,7 @@
             pltpu.VMEM((far, piece, hid), F32),
             pltpu.VMEM((far, piece, hid), F32),
             pltpu.VMEM((rows, hid), BF16),
-            dma((2,)), dma((2,)), dma((2,)), dma((2,)),
+            dma((6,)), dma((6,)), dma((2,)), dma((2,)),
             dma((7,)), dma((7,)), dma((7,)), dma((7,)), dma((far,)), dma((far,)),
         ],
         compiler_params=pltpu.CompilerParams(

time: 55.9 us -> 52.9 us (0.946)
  Pallas kernels: 45.8 us -> 42.8 us
    pallas_call x1, Pallas kernels: 45.8 us -> 42.8 us  [local(): pl.pallas_call(functools.partial(kernel, space_size, cfg), out_shape=(jax...]
where the time goes in v3:
time: 52.9 us; the launch traced here: 52.7 us
  Pallas kernels  42.8 us (81%)
  local copies, waits for them, and re-layouts  7.82 us (15%)
  other arithmetic  1.23 us (2%)
  between operations  0.81 us (2%)
    pallas_call x1, Pallas kernels, local(): pl.pallas_call(functools.partial(kernel, space_size, cfg), out_shape=(jax...  42.8 us
    unnamed x17, local copies, waits for them, and re-layouts  2.88 us
    reshape x2, local copies, waits for them, and re-layouts, local(): state.reshape(2, cp, own, lon)[:, :C].transpose(1, 0, 2, 3)  1.21 us

profile of v3, /device:TPU:0, one launch (start us, length us, event | category | flops | bytes accessed | tf_op | source)
XLA Modules:
  0.0 52.7 jit_solution(17116947429899835610)
XLA Ops:
  0.7 0.0 copy-start.6
  0.7 0.1 slice_multiply_fusion
  0.8 0.5 %copy-done.6 = s32[2]{0:T(128)S(1)} copy-done((s32[2]{0:T(128)S(1)}, s32[2]{0:T(128)}, u32[]{:S(2)}) %copy-start.6) | copy-done | bytes 32
  1.3 0.6 %copy-done.7 = f32[78]{0:T(128)S(1)} copy-done((f32[78]{0:T(128)S(1)}, f32[78]{0:T(128)}, u32[]{:S(2)}) %copy-start.7) | copy-done | bytes 336
  2.0 0.1 pad_maximum_fusion
  2.1 0.1 broadcast_in_dim.8.seeds
  2.1 0.8 %slice.40 = bf16[9,128,8]{1,2,0:T(8,128)(2,1)S(1)} slice(bf16[9,128,86]{1,2,0:T(8,128)(2,1)} %param.10), slice={[0:9], [0:128], [78:86]} | slice | bytes 36864 | tf_op jit(solution)/shard_map/slice | solution.py:423
  3.0 0.1 broadcast_in_dim.9.aux
  3.1 0.1 copy.23.w1n
  3.2 0.1 copy.25.b2
  3.3 0.0 copy-done.4
  3.3 0.1 copy.24.b1
  3.4 0.0 copy-done.3
  3.4 0.1 fusion.2
  3.6 0.0 copy-start.1
  3.6 0.9 %copy-done.1 = bf16[9,78,128]{2,1,0:T(8,128)(2,1)S(1)} copy-done((bf16[9,78,128]{2,1,0:T(8,128)(2,1)S(1)}, bf16[9,78,128]{2,1,0:T(8,128)(2,1)}, u32[]{:S(2)}) %copy-start.1) | copy-done | bytes 179736
  4.5 0.1 fusion.4
  4.5 0.0 copy-start
  4.5 0.0 copy-start.5
  4.6 0.1 copy.26.w2t
  4.7 0.8 %copy-done = bf16[9,128,86]{1,2,0:T(8,128)(2,1)S(1)} copy-done((bf16[9,128,86]{1,2,0:T(8,128)(2,1)S(1)}, bf16[9,128,86]{1,2,0:T(8,128)(2,1)}, u32[]{:S(2)}) %copy-start) | copy-done | bytes 198168
  5.5 0.1 fusion.3
  5.6 0.1 copy.22.w1s
  5.8 42.8 %shard_map.110 = (f32[1536,128]{1,0:T(8,128)S(1)}, f32[2,80,512]{2,1,0:T(8,128)S(1)}) custom-call(bf16[160,1024]{1,0:T(8,128)(2,1)S(1)} %bitcast.42, s32[8,128]{1,0:T(8,128)S(1)} %broadcast_in_dim.8.seeds, f32[24,256]{1,0:T(8,128)S(1)} %broadcast_in_dim.9.aux, bf16[3,128,240]{2,1,0:T(8,128)(2,1)S(1)} %copy.22.w1s, bf16[128,144]{1,0:T(8,128)(2,1)S(1)} %copy.23.w1n, ...), custom_call_target="tpu_custom_call" | custom-call | tf_op jit(solution)/shard_map/pallas_call | solution.py:440
  48.6 0.2 reshape.56
  48.8 0.1 slice_bitcast_fusion
  49.0 0.1 copy.27
  49.1 1.0 %reshape.57 = f32[78,4,256]{2,1,0:T(4,128)} reshape(f32[78,2,2,256]{3,2,1,0:T(2,128)S(1)} %copy.27) | data formatting | bytes 638976 | tf_op jit(solution)/shard_map/reshape | solution.py:475
  50.1 0.5 slice_bitcast_fusion.2
  50.6 0.8 %slice.46 = f32[720,128]{1,0:T(8,128)} slice(f32[1536,128]{1,0:T(8,128)S(1)} %get-tuple-element.8), slice={[792:1512], [0:128]} | slice | bytes 737280 | tf_op jit(solution)/shard_map/slice | solution.py:481
  51.4 0.5 slice_bitcast_fusion.1
  51.9 0.8 %maximum_bitcast_fusion = f32[9,128,86]{1,2,0:T(8,128)} fusion(f32[9,8,128]{2,1,0:T(8,128)S(1)} %slice.51, f32[9,78,128]{2,1,0:T(8,128)S(1)} %slice.50), kind=kLoop, calls=%fused_computation.3 | loop fusion | flops 99072 | bytes 792576 | tf_op jit(solution)/shard_map/transpose | solution.py:479
  (18 shorter events, 0.2 us)
Async XLA Ops:
  0.7 0.7 %copy-start.6 = (s32[2]{0:T(128)S(1)}, s32[2]{0:T(128)}, u32[]{:S(2)}) copy-start(s32[2]{0:T(128)} %param.9) | copy-start | bytes 28
  1.3 0.7 %copy-start.7 = (f32[78]{0:T(128)S(1)}, f32[78]{0:T(128)}, u32[]{:S(2)}) copy-start(f32[78]{0:T(128)} %param.13) | copy-start | bytes 940
  2.1 1.2 %copy-start.4 = (f32[128]{0:T(128)S(1)}, f32[128]{0:T(128)}, u32[]{:S(2)}) copy-start(f32[128]{0:T(128)} %param.11) | copy-start | bytes 1540
  2.1 1.3 %copy-start.2 = (bf16[78,4,256]{2,1,0:T(4,128)(2,1)S(1)}, bf16[78,4,256]{2,1,0:T(4,128)(2,1)}, u32[]{:S(2)}) copy-start(bf16[78,4,256]{2,1,0:T(4,128)(2,1)} %param.8) | copy-start | bytes 479236
  2.1 1.3 %copy-start.3 = (bf16[78,4,256]{2,1,0:T(4,128)(2,1)S(1)}, bf16[78,4,256]{2,1,0:T(4,128)(2,1)}, u32[]{:S(2)}) copy-start(bf16[78,4,256]{2,1,0:T(4,128)(2,1)} %param.7) | copy-start | bytes 479236
  3.6 0.9 %copy-start.1 = (bf16[9,78,128]{2,1,0:T(8,128)(2,1)S(1)}, bf16[9,78,128]{2,1,0:T(8,128)(2,1)}, u32[]{:S(2)}) copy-start(bf16[9,78,128]{2,1,0:T(8,128)(2,1)} %param.12) | copy-start | bytes 539140
  4.5 0.9 %copy-start = (bf16[9,128,86]{1,2,0:T(8,128)(2,1)S(1)}, bf16[9,128,86]{1,2,0:T(8,128)(2,1)}, u32[]{:S(2)}) copy-start(bf16[9,128,86]{1,2,0:T(8,128)(2,1)} %param.10) | copy-start | bytes 594436
  4.5 0.9 %copy-start.5 = (pred[80]{0:T(512)(128)(4,1)S(1)}, pred[80]{0:T(512)(128)(4,1)}, u32[]{:S(2)}) copy-start(pred[80]{0:T(512)(128)(4,1)} %constant.34.clone.1) | copy-start | bytes 244

commit v4 on v3

--- a/solution.py
+++ b/solution.py
@@ -333,9 +333,9 @@
             device_id=quad_peers[d - 1], device_id_type=MESH,
         ))
         copies[-1].start()
-    state_copy.start()
     for copy in copies:
         copy.wait()
+    state_copy.start()
     keep2 = pl.multiple_of(keep1 + quad * quarter, quarter)
     value = total[pl.ds(keep2, quarter), :]
     for d in range(3):

time: 52.9 us -> 52.5 us (level)
  no operation moved by 1% of the time
where the time goes in v4:
time: 52.5 us; the launch traced here: 52.3 us
  Pallas kernels  42.4 us (81%)
  local copies, waits for them, and re-layouts  7.82 us (15%)
  other arithmetic  1.23 us (2%)
  between operations  0.81 us (2%)
    pallas_call x1, Pallas kernels, local(): pl.pallas_call(functools.partial(kernel, space_size, cfg), out_shape=(jax...  42.4 us
    unnamed x17, local copies, waits for them, and re-layouts  2.88 us
    reshape x2, local copies, waits for them, and re-layouts, local(): state.reshape(2, cp, own, lon)[:, :C].transpose(1, 0, 2, 3)  1.21 us

profile of v4, /device:TPU:0, one launch (start us, length us, event | category | flops | bytes accessed | tf_op | source)
XLA Modules:
  0.0 52.3 jit_solution(18313089217239425329)
XLA Ops:
  0.7 0.0 copy-start.6
  0.7 0.1 slice_multiply_fusion
  0.8 0.5 %copy-done.6 = s32[2]{0:T(128)S(1)} copy-done((s32[2]{0:T(128)S(1)}, s32[2]{0:T(128)}, u32[]{:S(2)}) %copy-start.6) | copy-done | bytes 32
  1.3 0.6 %copy-done.7 = f32[78]{0:T(128)S(1)} copy-done((f32[78]{0:T(128)S(1)}, f32[78]{0:T(128)}, u32[]{:S(2)}) %copy-start.7) | copy-done | bytes 336
  2.0 0.1 pad_maximum_fusion
  2.1 0.1 broadcast_in_dim.8.seeds
  2.1 0.8 %slice.40 = bf16[9,128,8]{1,2,0:T(8,128)(2,1)S(1)} slice(bf16[9,128,86]{1,2,0:T(8,128)(2,1)} %param.10), slice={[0:9], [0:128], [78:86]} | slice | bytes 36864 | tf_op jit(solution)/shard_map/slice | solution.py:423
  3.0 0.1 broadcast_in_dim.9.aux
  3.1 0.1 copy.23.w1n
  3.2 0.1 copy.25.b2
  3.3 0.0 copy-done.4
  3.3 0.1 copy.24.b1
  3.4 0.0 copy-done.2
  3.4 0.1 fusion.2
  3.6 0.0 copy-start.1
  3.6 0.9 %copy-done.1 = bf16[9,78,128]{2,1,0:T(8,128)(2,1)S(1)} copy-done((bf16[9,78,128]{2,1,0:T(8,128)(2,1)S(1)}, bf16[9,78,128]{2,1,0:T(8,128)(2,1)}, u32[]{:S(2)}) %copy-start.1) | copy-done | bytes 179736
  4.5 0.1 fusion.4
  4.5 0.0 copy-start
  4.5 0.0 copy-start.5
  4.6 0.1 copy.26.w2t
  4.7 0.8 %copy-done = bf16[9,128,86]{1,2,0:T(8,128)(2,1)S(1)} copy-done((bf16[9,128,86]{1,2,0:T(8,128)(2,1)S(1)}, bf16[9,128,86]{1,2,0:T(8,128)(2,1)}, u32[]{:S(2)}) %copy-start) | copy-done | bytes 198168
  5.5 0.1 fusion.3
  5.6 0.1 copy.22.w1s
  5.8 42.4 %shard_map.110 = (f32[1536,128]{1,0:T(8,128)S(1)}, f32[2,80,512]{2,1,0:T(8,128)S(1)}) custom-call(bf16[160,1024]{1,0:T(8,128)(2,1)S(1)} %bitcast.42, s32[8,128]{1,0:T(8,128)S(1)} %broadcast_in_dim.8.seeds, f32[24,256]{1,0:T(8,128)S(1)} %broadcast_in_dim.9.aux, bf16[3,128,240]{2,1,0:T(8,128)(2,1)S(1)} %copy.22.w1s, bf16[128,144]{1,0:T(8,128)(2,1)S(1)} %copy.23.w1n, ...), custom_call_target="tpu_custom_call" | custom-call | tf_op jit(solution)/shard_map/pallas_call | solution.py:440
  48.2 0.2 reshape.56
  48.4 0.1 slice_bitcast_fusion
  48.5 0.1 copy.27
  48.6 1.0 %reshape.57 = f32[78,4,256]{2,1,0:T(4,128)} reshape(f32[78,2,2,256]{3,2,1,0:T(2,128)S(1)} %copy.27) | data formatting | bytes 638976 | tf_op jit(solution)/shard_map/reshape | solution.py:475
  49.6 0.5 slice_bitcast_fusion.2
  50.1 0.8 %slice.46 = f32[720,128]{1,0:T(8,128)} slice(f32[1536,128]{1,0:T(8,128)S(1)} %get-tuple-element.8), slice={[792:1512], [0:128]} | slice | bytes 737280 | tf_op jit(solution)/shard_map/slice | solution.py:481
  50.9 0.5 slice_bitcast_fusion.1
  51.5 0.8 %maximum_bitcast_fusion = f32[9,128,86]{1,2,0:T(8,128)} fusion(f32[9,8,128]{2,1,0:T(8,128)S(1)} %slice.51, f32[9,78,128]{2,1,0:T(8,128)S(1)} %slice.50), kind=kLoop, calls=%fused_computation.3 | loop fusion | flops 99072 | bytes 792576 | tf_op jit(solution)/shard_map/transpose | solution.py:479
  (18 shorter events, 0.2 us)
Async XLA Ops:
  0.7 0.7 %copy-start.6 = (s32[2]{0:T(128)S(1)}, s32[2]{0:T(128)}, u32[]{:S(2)}) copy-start(s32[2]{0:T(128)} %param.9) | copy-start | bytes 28
  1.3 0.7 %copy-start.7 = (f32[78]{0:T(128)S(1)}, f32[78]{0:T(128)}, u32[]{:S(2)}) copy-start(f32[78]{0:T(128)} %param.13) | copy-start | bytes 940
  2.1 1.2 %copy-start.4 = (f32[128]{0:T(128)S(1)}, f32[128]{0:T(128)}, u32[]{:S(2)}) copy-start(f32[128]{0:T(128)} %param.11) | copy-start | bytes 1540
  2.1 1.3 %copy-start.2 = (bf16[78,4,256]{2,1,0:T(4,128)(2,1)S(1)}, bf16[78,4,256]{2,1,0:T(4,128)(2,1)}, u32[]{:S(2)}) copy-start(bf16[78,4,256]{2,1,0:T(4,128)(2,1)} %param.8) | copy-start | bytes 479236
  2.1 1.3 %copy-start.3 = (bf16[78,4,256]{2,1,0:T(4,128)(2,1)S(1)}, bf16[78,4,256]{2,1,0:T(4,128)(2,1)}, u32[]{:S(2)}) copy-start(bf16[78,4,256]{2,1,0:T(4,128)(2,1)} %param.7) | copy-start | bytes 479236
  3.6 0.9 %copy-start.1 = (bf16[9,78,128]{2,1,0:T(8,128)(2,1)S(1)}, bf16[9,78,128]{2,1,0:T(8,128)(2,1)}, u32[]{:S(2)}) copy-start(bf16[9,78,128]{2,1,0:T(8,128)(2,1)} %param.12) | copy-start | bytes 539140
  4.5 0.9 %copy-start = (bf16[9,128,86]{1,2,0:T(8,128)(2,1)S(1)}, bf16[9,128,86]{1,2,0:T(8,128)(2,1)}, u32[]{:S(2)}) copy-start(bf16[9,128,86]{1,2,0:T(8,128)(2,1)} %param.10) | copy-start | bytes 594436
  4.5 0.9 %copy-start.5 = (pred[80]{0:T(512)(128)(4,1)S(1)}, pred[80]{0:T(512)(128)(4,1)}, u32[]{:S(2)}) copy-start(pred[80]{0:T(512)(128)(4,1)} %constant.34.clone.1) | copy-start | bytes 244
